TPU v7x, 1024 devices: a whole 8x8x8 slice. The times are simulated.
1024 devices in a mesh: node: 64 (over z_hi, x, core), local: 16 (over y, z_lo).
Axes of the slice: x: 8, y: 8, z: 8 (z_hi: 4, z_lo: 2; z = z_hi * 2 + z_lo), core: 2. Of those that a mesh axis runs over, the one named last changes fastest.
Arguments:
- tokens: bfloat16 [5632, 4096], P('local', 'node'), may hold values from -16 to 16
- codes: bfloat16 [4096, 2, 11008], P('local', None, 'node'), may hold values from -1 to 1
- scales: bfloat16 [4096, 2], P('local'), may hold values from 0.0078125 to 0.078125
- cotangent: bfloat16 [5632, 11008], P('local', 'node'), may hold values from -0.079589844 to 0.079589844
Outputs:
- hidden: bfloat16 [5632, 11008], P('local', 'node')
- grads: float32 [4096, 2, 11008], P('local', None, 'node')
All inputs are finite; a program needn't handle non-finite values.
Results may differ from a plain program's by a relative error of at most 0.02.
Values may be sent and summed in bfloat16 or wider, within the bound.
A program may use at most 32 MiB of HBM per device.

v0:
```python
import jax
import jax.numpy as jnp
from jax import lax
from jax.sharding import PartitionSpec as P


def body(tokens, codes, scales, cotangent):
    width = codes.shape[2]
    full_tokens = lax.all_gather(tokens, "node", axis=1, tiled=True)
    full_codes, full_scales = (
        lax.all_gather(codes, "local", axis=0, tiled=True),
        lax.all_gather(scales, "local", axis=0, tiled=True),
    )
    rows = full_codes.shape[0]
    count_tok = full_tokens.shape[0]
    scaled = full_codes.astype(jnp.float32) * full_scales.astype(jnp.float32)[:, :, None]
    weights = scaled.astype(jnp.bfloat16).reshape(rows, 2 * width)
    both = jnp.dot(full_tokens, weights, preferred_element_type=jnp.float32).reshape(
        count_tok, 2, width
    )
    gate = both[:, 0, :]
    up = both[:, 1, :]
    sig = jax.nn.sigmoid(gate)
    silu_gate = gate * sig
    hidden = (silu_gate * up).astype(jnp.bfloat16)
    grad_h = cotangent.astype(jnp.float32)
    dgate = grad_h * up * sig * (1.0 + gate * (1.0 - sig))
    dup = grad_h * silu_gate
    dboth = jnp.stack([dgate, dup], axis=1).astype(jnp.bfloat16).reshape(count_tok, 2 * width)
    term = lax.dot_general(
        full_tokens, dboth, (((0,), (0,)), ((), ())), preferred_element_type=jnp.float32
    )
    summed = lax.psum_scatter(
        term.astype(jnp.bfloat16), "local", scatter_dimension=0, tiled=True
    ).astype(jnp.float32)
    grads = summed.reshape(summed.shape[0], 2, width)
    return (hidden, grads)


def solution(mesh):
    in_specs = (P("local", "node"), P("local", None, "node"), P("local", None), P("local", "node"))
    out_specs = (P("local", "node"), P("local", None, "node"))
    return jax.shard_map(body, mesh=mesh, in_specs=in_specs, out_specs=out_specs, check_vma=False)
```

profile of v0, /device:TPU:4, one launch (start us, length us, event | category | flops | bytes accessed | tf_op | source)
XLA Modules:
  0.0 322.6 jit_solution(181982085623288580)
XLA Ops:
  7.2 0.0 all-gather.3.cloned.1.call-start
  7.2 0.7 all-gather.3.cloned.1.call-update
  7.9 0.0 all-gather.5.cloned.1.call-start
  7.9 0.7 all-gather.5.cloned.1.call-update
  8.6 0.0 reduce-scatter.2.cloned.1.call-start
  8.7 36.8 %all_gather.10 = bf16[4096,2]{0,1:T(2,128)(2,1)S(1)} all-gather(bf16[256,2]{0,1:T(2,128)(2,1)} %param.6), channel_id=1, replica_groups=mesh['node'=64,'local'=16] {'local'}, dimensions={0}, use_global_device_ids=true | all-gather | bytes 17408 | tf_op jit(solution)/shard_map/all_gather | solution.py:12
  45.5 83.5 %all-gather.3.cloned.1.call-done = bf16[4096,2,172]{0,1,2:T(2,128)(2,1)} async-done(((bf16[256,2,172]{0,1,2:T(2,128)(2,1)}), bf16[4096,2,172]{0,1,2:T(2,128)(2,1)}) %all-gather.3.cloned.1.call-update) | async-done | bytes 2818064 | tf_op jit(solution)/shard_map/all_gather | solution.py:11
  129.1 4.7 %multiply_convert_fusion = bf16[4096,2,172]{0,1,2:T(2,128)(2,1)S(1)} fusion(bf16[4096,2,172]{0,1,2:T(2,128)(2,1)} %all-gather.3.cloned.1.call-done, f32[4096,2]{0,1:T(2,128)S(1)} %convert_element_type.28), kind=kLoop, calls=%fused_computation | loop fusion | flops 4227072 | bytes 5668864 | tf_op jit(solution)/shard_map/convert_element_type | solution.py:17
  133.8 1.9 copy.7
  135.7 2.1 reshape.20
  137.8 0.0 copy-start
  137.8 83.6 %all-gather.5.cloned.1.call-done = bf16[352,4096]{0,1:T(8,128)(2,1)} async-done(((bf16[352,64]{0,1:T(8,128)(2,1)}), bf16[352,4096]{0,1:T(8,128)(2,1)}) %all-gather.5.cloned.1.call-update) | async-done | bytes 2883600 | tf_op jit(solution)/shard_map/all_gather | solution.py:9
  221.4 4.4 %convolution_bitcast_fusion = f32[352,344]{0,1:T(8,128)S(1)} fusion(bf16[4096,344]{0,1:T(8,128)(2,1)} %reshape.20, bf16[352,4096]{0,1:T(8,128)(2,1)} %all-gather.5.cloned.1.call-done), kind=kOutput, calls=%fused_computation.3 | convolution fusion | flops 991952896 | bytes 6185984 | tf_op jit(solution)/shard_map/dot_general | solution.py:18
  225.8 0.1 reshape.21
  225.8 0.0 copy-done
  225.8 0.8 fusion.7
  226.7 0.1 pad_maximum_fusion
  226.7 0.1 convert_element_type.32
  226.8 5.1 %fusion = bf16[4096,344]{0,1:T(8,128)(2,1)} fusion(bf16[352,344]{0,1:T(8,128)(2,1)S(1)} %convert_element_type.32, bf16[352,4096]{0,1:T(8,128)(2,1)} %all-gather.5.cloned.1.call-done), kind=kOutput, calls=%fused_computation.2 | convolution fusion | flops 993361920 | bytes 5943808 | tf_op jit(solution)/shard_map/dot_general | solution.py:30
  231.9 0.0 reduce-scatter.2.cloned.1.call-update
  232.0 82.1 %reduce-scatter.2.cloned.1.call-done = bf16[256,344]{0,1:T(8,128)(2,1)} async-done(((bf16[4096,344]{0,1:T(8,128)(2,1)}), bf16[256,344]{0,1:T(8,128)(2,1)}) %reduce-scatter.2.cloned.1.call-update) | async-done | bytes 176144 | tf_op jit(solution)/shard_map/reduce_scatter | solution.py:33
  314.1 1.0 reshape.25
  315.0 1.0 copy.8
  (1 shorter events, 0.0 us)
Async XLA Ops:
  7.2 121.9 %all-gather.3.cloned.1.call-start = ((), (), s32[]{:S(2)}) async-start(), calls=%async_computation.1 | async-start | bytes 2994176 | tf_op jit(solution)/shard_map/all_gather | solution.py:11
  7.9 213.5 %all-gather.5.cloned.1.call-start = ((), (), s32[]{:S(2)}) async-start(), calls=%async_computation.2 | async-start | bytes 3194880 | tf_op jit(solution)/shard_map/all_gather | solution.py:9
  8.6 305.4 %reduce-scatter.2.cloned.1.call-start = ((), (), s32[]{:S(2)}) async-start(), calls=%async_computation.3 | async-start | bytes 2994176 | tf_op jit(solution)/shard_map/reduce_scatter | solution.py:33
  137.8 88.0 %copy-start = (bf16[352,172]{0,1:T(8,128)(2,1)S(1)}, bf16[352,172]{0,1:T(8,128)(2,1)}, u32[]{:S(2)}) copy-start(bf16[352,172]{0,1:T(8,128)(2,1)} %param.7) | copy-start | bytes 363268
Sparse Core Ops, SparseCore 0:
  10.6 118.4 all-gather.2
  133.5 87.8 all-gather.4
  232.1 81.9 reduce-scatter.1
where the time goes:
time: 323 us
  waiting for transfers between devices  251 us (78%)
  blocking collectives  36.8 us (11%)
  between operations  13.8 us (4%)
  matrix products  9.48 us (3%)
  local copies, waits for them, and re-layouts  6.08 us (2%)
  other arithmetic  5.6 us (2%)
    all_gather x1, waiting for transfers between devices, body(): full_tokens = lax.all_gather(tokens, 'node', axis=1, tiled=True)  83.6 us
    all_gather x1, waiting for transfers between devices, body(): lax.all_gather(codes, 'local', axis=0, tiled=True)  83.5 us
    reduce_scatter x1, waiting for transfers between devices, body(): lax.psum_scatter(term.astype(jnp.bfloat16), 'local', scatter_dimension=0,...  82.1 us
    all_gather x1, blocking collectives, body(): lax.all_gather(scales, 'local', axis=0, tiled=True)  36.8 us
  transfers between devices with their start and end apart: 3, of which 3 were waited for; matrix products, arithmetic and copies ran while one was open for 3% of the time, Pallas kernels for 0%

commit v1 on v0

v1 whole, which is shorter than its diff:
```python
import jax
import jax.numpy as jnp
from jax import lax
from jax.experimental import pallas as pl
from jax.experimental.pallas import tpu as pltpu
from jax.sharding import PartitionSpec as P

MESH = pl.DeviceIdType.MESH
F32 = jnp.float32
BF16 = jnp.bfloat16
TOK = 352
FEAT = 64
HALF = 88
ROWS = 2 * HALF
KB = 256
D = 4096
RING = 8

EVENTS = [
    ("a", 1), ("a", 2), ("b", 0, 1), ("o", 1), ("b", 1, 1), ("w",), ("b", -1, 1), ("a", 3), ("a", 4),
    ("b", 2, 1), ("b", -2, 1), ("o", 2), ("b", 0, 2), ("b", 1, 2), ("b", -1, 2), ("b", 3, 1), ("p", 1),
    ("b", -3, 1), ("b", 4, 1), ("b", 2, 2), ("o", 3), ("b", -2, 2), ("b", 0, 3), ("b", 1, 3), ("b", -1, 3),
    ("p", 2), ("b", 3, 2), ("b", -3, 2), ("b", 4, 2), ("o", 4), ("b", 2, 3), ("b", -2, 3), ("b", 0, 4),
    ("b", 1, 4), ("b", -1, 4), ("b", 3, 3), ("p", 3), ("b", -3, 3), ("b", 4, 3), ("b", 2, 4), ("b", -2, 4),
    ("b", 3, 4), ("b", -3, 4), ("b", 4, 4),
]


def kernel(
    tok_ref, w_ref, cot_ref, hid_out, grad_out,
    tt, wb, ct, cot_send, hb, hid_recv, both, dbt, rs_send, rs_recv, fin_send, fin_recv,
    a_s, a_r, b_s, b_r, sib_s, sib_r, y_s, y_r, one_s, one_r, g_s, g_r,
):
    node, local = lax.axis_index("node"), lax.axis_index("local")
    core = node % 2
    x = (node // 2) % 8
    z_lo = local % 2
    z = (node // 16) * 2 + z_lo
    y = local // 2

    def wrap(v):
        return (v + RING) % RING

    def device(cx, cy, cz, cc):
        return ((cz // 2) * 16 + cx * 2 + cc, cy * 2 + cz % 2)

    first, second = jnp.where(core == 0, x, z), jnp.where(core == 0, z, x)

    def at(a, b):
        return jnp.where(core == 0, a, b), jnp.where(core == 0, b, a)

    def on_first(step):
        cx, cz = at(wrap(first + step), second)
        return device(cx, y, cz, core)

    def on_second(step):
        cx, cz = at(first, wrap(second + step))
        return device(cx, y, cz, core)

    def on_y(step):
        return device(x, wrap(y + step), z, core)

    sibling = device(x, y, z, 1 - core)
    partner = device(x, y, (z // 2) * 2 + (1 - z_lo), core)

    def rows_of(a, b, lo=0):
        cx, cz = at(wrap(first + a), wrap(second + b))
        return pl.multiple_of(((cz % 2) * 64 + (cz // 2) * 16 + cx * 2 + core) * FEAT + lo, 16)

    def block(a, b, part=None):
        if part is None:
            return tt.at[pl.ds(rows_of(a, b), FEAT), :]
        return tt.at[pl.ds(rows_of(a, b, 32 * part), 32), :]

    sent = []

    def copy(src, dst, send, recv, target):
        return pltpu.make_async_remote_copy(
            src_ref=src, dst_ref=dst, send_sem=send, recv_sem=recv, device_id=target, device_id_type=MESH
        )

    def send(*args):
        c = copy(*args)
        c.start()
        sent.append(c)

    barrier = pltpu.get_barrier_semaphore()
    peers = [on_first(1), on_first(-1), on_first(2), on_first(-2), on_second(1), on_second(-1), on_y(1), on_y(-1), sibling]
    for peer in peers:
        pl.semaphore_signal(barrier, inc=1, device_id=peer, device_id_type=MESH)

    own = rows_of(0, 0)
    tt[pl.ds(own, FEAT), :] = tok_ref[...]
    mine = 2 * y + z_lo
    theirs = 2 * y + 1 - z_lo
    wb[mine] = w_ref[pl.ds(pl.multiple_of(z_lo * ROWS, 16), ROWS), :]

    def halves(v, width):
        low = v[0:HALF]
        high = jnp.concatenate([v[HALF:172], jnp.zeros((4, width), F32)], axis=0)
        return low, high

    low, high = halves(cot_ref[...].astype(F32), TOK)
    pad = jnp.zeros((8, TOK), F32)
    keep = jnp.where(z_lo == 0, low, high)
    give = jnp.where(z_lo == 0, high, low)
    ct[z_lo] = jnp.concatenate([keep, pad], axis=0).astype(BF16)
    cot_send[...] = jnp.concatenate([give, pad], axis=0).astype(BF16)
    pl.semaphore_wait(barrier, len(peers))

    def a_copy(way, dist):
        sign = 1 - 2 * way
        k = way * 4 + dist - 1
        if dist <= 2:
            src, hops, part = (0, 0), dist, None
        elif dist == 3:
            src, hops, part = (-2 * sign, 0), 1, None
        else:
            src, hops, part = (-2 * sign, 0), 2, way
        ref = block(*src, part)
        return copy(ref, ref, a_s.at[k], a_r.at[k], on_first(sign * hops))

    def a_arrives(way, dist):
        sign = 1 - 2 * way
        k = way * 4 + dist - 1
        ref = block(-sign * dist, 0, way if dist == 4 else None)
        copy(ref, ref, a_s.at[k], a_r.at[k], on_first(sign)).wait_recv()

    def b_index(way, item, step):
        return (way * 8 + item + 3) * 4 + step - 1

    def b_send(way, item, step):
        sign = 1 - 2 * way
        k = b_index(way, item, step)
        ref = block(item, -sign * (step - 1), way if step == 4 else None)
        send(ref, ref, b_s.at[k], b_r.at[k], on_second(sign))

    def b_arrives(way, item, step):
        sign = 1 - 2 * way
        k = b_index(way, item, step)
        ref = block(item, -sign * step, way if step == 4 else None)
        copy(ref, ref, b_s.at[k], b_r.at[k], on_second(sign)).wait_recv()

    def share(a, b):
        k = (a + 3) * 8 + b + 3
        ref = block(a, b)
        send(ref, ref, sib_s.at[k], sib_r.at[k], sibling)

    def y_index(way, kind, step):
        return (way * 2 + kind) * 4 + step - 1

    def y_block(kind, offset):
        return wb.at[2 * wrap(y + offset) + (z_lo if kind == 0 else 1 - z_lo)]

    def y_send(way, kind, step):
        sign = 1 - 2 * way
        k = y_index(way, kind, step)
        ref = y_block(kind, -sign * (step - 1))
        send(ref, ref, y_s.at[k], y_r.at[k], on_y(sign))

    def y_arrives(way, kind, step):
        sign = 1 - 2 * way
        k = y_index(way, kind, step)
        ref = y_block(kind, -sign * step)
        copy(ref, ref, y_s.at[k], y_r.at[k], on_y(sign)).wait_recv()

    def y_steps(way, kind):
        return 4 if way == kind else 3

    for way in range(2):
        for dist in (1, 2):
            c = a_copy(way, dist)
            c.start()
            sent.append(c)
        b_send(way, 0, 1)
        y_send(way, 0, 1)
    w_other = w_ref.at[pl.ds(pl.multiple_of((1 - z_lo) * ROWS, 16), ROWS), :]
    send(w_other, wb.at[mine], one_s.at[0], one_r.at[0], partner)
    share(0, 0)
    send(cot_send, ct.at[z_lo], one_s.at[1], one_r.at[1], partner)

    for event in EVENTS:
        if event[0] == "a":
            dist = event[1]
            for way in range(2):
                a_arrives(way, dist)
                if dist == 2:
                    for far in (3, 4):
                        c = a_copy(way, far)
                        c.start()
                        sent.append(c)
            for item in ((-dist, dist) if dist < 4 else (4,)):
                for way in range(2):
                    b_send(way, item, 1)
                share(item, 0)
        elif event[0] == "b":
            _, item, step = event
            for way in range(2):
                b_arrives(way, item, step)
                if step < 4:
                    b_send(way, item, step + 1)
            if step < 4:
                share(item, -step)
                share(item, step)
            else:
                share(item, 4)
        elif event[0] == "w":
            copy(w_other, wb.at[theirs], one_s.at[0], one_r.at[0], partner).wait_recv()
            for way in range(2):
                y_send(way, 1, 1)
        else:
            kind, step = (0 if event[0] == "o" else 1), event[1]
            for way in range(2):
                if step <= y_steps(way, kind):
                    y_arrives(way, kind, step)
                    if step < y_steps(way, kind):
                        y_send(way, kind, step + 1)
    y_arrives(1, 1, 4)
    copy(cot_send, ct.at[1 - z_lo], one_s.at[1], one_r.at[1], partner).wait_recv()

    def sib_arrives(a, b):
        k = (a + 3) * 8 + b + 3
        cz = jnp.where(core == 0, wrap(z + a), wrap(z + b))
        cx = jnp.where(core == 0, wrap(x + b), wrap(x + a))
        r = pl.multiple_of(((cz % 2) * 64 + (cz // 2) * 16 + cx * 2 + 1 - core) * FEAT, 16)
        ref = tt.at[pl.ds(r, FEAT), :]
        copy(ref, ref, sib_s.at[k], sib_r.at[k], sibling).wait_recv()

    for a in range(-3, 5):
        for b in range(-3, 5):
            sib_arrives(a, b)

    for m in range(2):
        acc = jnp.zeros((ROWS, TOK), F32)
        for k in range(8):
            w = jnp.concatenate([wb[2 * k], wb[2 * k + 1]], axis=1)
            acc += jnp.dot(w, tt[D * m + 512 * k : D * m + 512 * (k + 1), :], preferred_element_type=F32)
        for t in range(3):
            wide = min(128, TOK - 128 * t)
            both[t, :, 0:wide] = acc[:, 128 * t : 128 * t + wide]
        for t in range(3):
            wide = min(128, TOK - 128 * t)
            gate = both[t, pl.ds(0, HALF, stride=2), :][:, 0:wide]
            up = both[t, pl.ds(1, HALF, stride=2), :][:, 0:wide]
            cot = ct[m, :, 128 * t : 128 * t + wide].astype(F32)[0:HALF]
            sig = jax.nn.sigmoid(gate)
            silu = gate * sig
            hid = jnp.concatenate([silu * up, jnp.zeros((8, wide), F32)], axis=0)
            hb[m, :, 128 * t : 128 * t + wide] = hid.astype(BF16)
            both[t, pl.ds(0, HALF, stride=2), 0:wide] = cot * up * sig * (1.0 + gate * (1.0 - sig))
            both[t, pl.ds(1, HALF, stride=2), 0:wide] = cot * silu
            dbt[m, :, 128 * t : 128 * t + wide] = both[t, :, 0:wide].astype(BF16)

    def partial(offset, kind):
        rows = 2 * wrap(y + offset) + (z_lo if kind == 0 else 1 - z_lo)
        off = pl.multiple_of(rows * KB, KB)
        total = jnp.zeros((ROWS, KB), F32)
        for m in range(2):
            total += lax.dot_general(
                dbt[m], tt[pl.ds(D * m + off, KB), :], (((1,), (1,)), ((), ())), preferred_element_type=F32
            )
        return total

    def g_copy(way, kind, step):
        k = y_index(way, kind, step)
        return copy(rs_send.at[k], rs_recv.at[k], g_s.at[k], g_r.at[k], on_y(1 - 2 * way))

    def arrived(way, kind, step):
        g_copy(way, kind, step).wait_recv()
        return rs_recv[y_index(way, kind, step)].astype(F32)

    for step in range(1, 5):
        for way, kind in ((0, 0), (1, 1), (0, 1), (1, 0)):
            steps = y_steps(way, kind)
            if step > steps:
                continue
            total = partial((1 - 2 * way) * (steps + 1 - step), kind)
            if step > 1:
                total += arrived(way, kind, step - 1)
            rs_send[y_index(way, kind, step)] = total.astype(BF16)
            c = g_copy(way, kind, step)
            c.start()
            sent.append(c)
        if step == 1:
            send(hb.at[1 - z_lo], hid_recv, one_s.at[2], one_r.at[2], partner)
    final = partial(0, 1)
    final_own = partial(0, 0)
    final += arrived(0, 1, 3)
    final += arrived(1, 1, 4)
    fin_send[...] = final.astype(BF16)
    send(fin_send, fin_recv, one_s.at[3], one_r.at[3], partner)

    copy(hb.at[1 - z_lo], hid_recv, one_s.at[2], one_r.at[2], partner).wait_recv()
    here = hb[z_lo].astype(F32)
    there = hid_recv[...].astype(F32)
    h_low = jnp.where(z_lo == 0, here, there)[0:HALF]
    h_high = jnp.where(z_lo == 0, there, here)[0 : 172 - HALF]
    hid_out[...] = jnp.concatenate([h_low, h_high], axis=0).astype(BF16)

    final_own += arrived(1, 0, 3)
    final_own += arrived(0, 0, 4)
    copy(fin_send, fin_recv, one_s.at[3], one_r.at[3], partner).wait_recv()
    other = fin_recv[...].astype(F32)
    grad_out[0:ROWS, :] = jnp.where(z_lo == 0, final_own, other)
    grad_out[ROWS:344, :] = jnp.where(z_lo == 0, other, final_own)[0 : 344 - ROWS]
    for c in sent:
        c.wait_send()


def body(tokens, codes, scales, cotangent):
    scaled = jnp.transpose(codes, (2, 1, 0)).astype(F32) * jnp.transpose(scales).astype(F32)[None]
    weights = jnp.pad(scaled.astype(BF16).reshape(344, KB), ((0, 8), (0, 0)))
    dma = pltpu.SemaphoreType.DMA
    vmem = pl.BlockSpec(memory_space=pltpu.VMEM)
    hidden, grads = pl.pallas_call(
        kernel,
        name="glu",
        out_shape=(jax.ShapeDtypeStruct((172, TOK), BF16), jax.ShapeDtypeStruct((344, KB), F32)),
        in_specs=[vmem] * 3,
        out_specs=(vmem, vmem),
        scratch_shapes=[
            pltpu.VMEM((2 * D, TOK), BF16),
            pltpu.VMEM((16, ROWS, KB), BF16),
            pltpu.VMEM((2, 96, TOK), BF16),
            pltpu.VMEM((96, TOK), BF16),
            pltpu.VMEM((2, 96, TOK), BF16),
            pltpu.VMEM((96, TOK), BF16),
            pltpu.VMEM((3, ROWS, 128), F32),
            pltpu.VMEM((2, ROWS, TOK), BF16),
            pltpu.VMEM((16, ROWS, KB), BF16),
            pltpu.VMEM((16, ROWS, KB), BF16),
            pltpu.VMEM((ROWS, KB), BF16),
            pltpu.VMEM((ROWS, KB), BF16),
            dma((8,)), dma((8,)), dma((64,)), dma((64,)), dma((64,)), dma((64,)),
            dma((16,)), dma((16,)), dma((4,)), dma((4,)), dma((16,)), dma((16,)),
        ],
        compiler_params=pltpu.CompilerParams(
            collective_id=0, has_side_effects=True, vmem_limit_bytes=40 * 2**20
        ),
    )(jnp.transpose(tokens), weights, jnp.transpose(cotangent))
    return jnp.transpose(hidden), jnp.transpose(grads.reshape(172, 2, KB), (2, 1, 0))


def solution(mesh):
    in_specs = (P("local", "node"), P("local", None, "node"), P("local", None), P("local", "node"))
    out_specs = (P("local", "node"), P("local", None, "node"))
    return jax.shard_map(body, mesh=mesh, in_specs=in_specs, out_specs=out_specs, check_vma=False)
```

time: 323 us -> 79 us (0.24)
  the two profiles are of different devices: /device:TPU:4 before, /device:TPU:2 now
where the time goes in v1:
time: 79 us; the launch traced here: 78.8 us
  Pallas kernels  73.8 us (93%)
  local copies, waits for them, and re-layouts  3.22 us (4%)
  other arithmetic  1.06 us (1%)
    pallas_call x1, Pallas kernels, body(): pl.pallas_call(kernel, name='glu', out_shape=(jax.ShapeDtypeStruct((172,...  73.8 us
    unnamed x7, local copies, waits for them, and re-layouts  2.2 us

profile of v1, /device:TPU:2, one launch (start us, length us, event | category | flops | bytes accessed | tf_op | source)
XLA Modules:
  0.0 78.8 jit_solution(13510263310251882702)
XLA Ops:
  0.6 0.0 copy-start.2
  0.6 0.7 copy-done.2
  1.3 1.1 %fusion = bf16[172,2,256]{2,1,0:T(2,128)(2,1)S(1)} fusion(bf16[256,2,172]{0,1,2:T(2,128)(2,1)} %param.5, f32[2,256]{1,0:T(2,128)S(1)} %convert_bitcast_fusion), kind=kLoop, calls=%fused_computation.1 | loop fusion | flops 264192 | bytes 354304 | tf_op jit(solution)/shard_map/convert_element_type | solution.py:312
  2.4 0.1 reshape.11
  2.5 0.0 copy-start
  2.5 0.0 copy-start.1
  2.5 0.9 %copy-done = bf16[352,172]{0,1:T(8,128)(2,1)S(1)} copy-done((bf16[352,172]{0,1:T(8,128)(2,1)S(1)}, bf16[352,172]{0,1:T(8,128)(2,1)}, u32[]{:S(2)}) %copy-start) | copy-done | bytes 121112
  3.4 0.0 copy-done.1
  3.4 73.8 %glu.1 = (bf16[172,352]{1,0:T(8,128)(2,1)S(1)}, f32[344,256]{1,0:T(8,128)S(1)}) custom-call(bf16[64,352]{1,0:T(8,128)(2,1)S(1)} %bitcast.12, bf16[352,256]{1,0:T(8,128)(2,1)S(1)} %pad.4.w_ref, bf16[172,352]{1,0:T(8,128)(2,1)S(1)} %bitcast.11), custom_call_target="tpu_custom_call" | custom-call | tf_op jit(solution)/shard_map/glu/pallas_call | solution.py:315
  77.2 0.9 %reshape.12 = f32[172,2,256]{2,1,0:T(2,128)} reshape(f32[344,256]{1,0:T(8,128)S(1)} %get-tuple-element.5) | data formatting | bytes 704512 | tf_op jit(solution)/shard_map/reshape | solution.py:341
  78.1 0.7 copy.7
  (2 shorter events, 0.0 us)
Async XLA Ops:
  0.6 0.7 copy-start.2
  2.5 0.9 %copy-start = (bf16[352,172]{0,1:T(8,128)(2,1)S(1)}, bf16[352,172]{0,1:T(8,128)(2,1)}, u32[]{:S(2)}) copy-start(bf16[352,172]{0,1:T(8,128)(2,1)} %param.7) | copy-start | bytes 363268
  2.5 0.9 %copy-start.1 = (bf16[352,64]{0,1:T(8,128)(2,1)S(1)}, bf16[352,64]{0,1:T(8,128)(2,1)}, u32[]{:S(2)}) copy-start(bf16[352,64]{0,1:T(8,128)(2,1)} %param.4) | copy-start | bytes 135172

commit v2 on v0

v2 whole, which is shorter than its diff:
```python
import jax
import jax.numpy as jnp
from jax import lax
from jax.experimental import pallas as pl
from jax.experimental.pallas import tpu as pltpu
from jax.sharding import PartitionSpec as P

MESH = pl.DeviceIdType.MESH
F32 = jnp.float32
BF16 = jnp.bfloat16
TOK = 352
FEAT = 64
HID = 172
HALF = 88
ROWS = 2 * HALF
KB = 256
RING = 8
BLOCK = 176
CUT = 96

FIRST = [
    ("+", "a", 2), ("+", "a", 1), ("+", "b", 0, 1),
]
STEPS = [
    ("-", "a", 2), ("+", "a", 3), ("+", "a", 4), ("+", "b", 2, 1), ("-", "a", 1), ("-", "w", 0), ("+", "b", -2, 1),
    ("-", "w", 1), ("+", "b", 1, 1), ("-", "o", 1, 0), ("+", "b", -1, 1), ("-", "b", 0, 1), ("+", "b", 0, 2),
    ("-", "o", 1, 1), ("-", "a", 3), ("+", "b", 3, 1), ("+", "b", -3, 1), ("-", "a", 4), ("+", "b", 4, 1),
    ("-", "p", 1, 0), ("-", "b", 2, 1), ("+", "b", 2, 2), ("-", "b", -2, 1), ("+", "b", -2, 2), ("-", "p", 1, 1),
    ("-", "b", 1, 1), ("+", "b", 1, 2), ("-", "b", -1, 1), ("+", "b", -1, 2), ("-", "o", 2, 0), ("-", "b", 0, 2),
    ("+", "b", 0, 3), ("-", "b", 3, 1), ("+", "b", 3, 2), ("-", "o", 2, 1), ("-", "b", -3, 1), ("+", "b", -3, 2),
    ("-", "b", 4, 1), ("+", "b", 4, 2), ("-", "p", 2, 0), ("-", "b", 2, 2), ("+", "b", 2, 3), ("-", "b", -2, 2),
    ("+", "b", -2, 3), ("-", "p", 2, 1), ("-", "b", 1, 2), ("+", "b", 1, 3), ("-", "b", -1, 2), ("+", "b", -1, 3),
    ("-", "o", 3, 0), ("-", "b", 0, 3), ("+", "b", 0, 4), ("-", "b", 3, 2), ("+", "b", 3, 3), ("-", "o", 3, 1),
    ("-", "b", -3, 2), ("+", "b", -3, 3), ("-", "b", 4, 2), ("+", "b", 4, 4), ("+", "b", 4, 3), ("-", "p", 3, 0),
    ("-", "b", 2, 3), ("+", "b", 2, 4), ("-", "b", -2, 3), ("+", "b", -2, 4), ("-", "p", 3, 1), ("-", "b", 1, 3),
    ("+", "b", 1, 4), ("-", "b", -1, 3), ("+", "b", -1, 4), ("-", "b", 0, 4), ("-", "o", 4, 0), ("-", "b", 3, 3),
    ("+", "b", 3, 4), ("-", "b", -3, 3), ("+", "b", -3, 4), ("-", "o", 4, 1), ("-", "p", 4, 0), ("-", "b", 4, 4),
    ("-", "b", 4, 3), ("-", "b", 2, 4), ("-", "p", 4, 1), ("-", "b", -2, 4), ("-", "b", 1, 4), ("-", "b", -1, 4),
    ("-", "b", 3, 4), ("-", "b", -3, 4),
]


def kernel(
    tok_hbm, codes_hbm, scales_hbm, cot_hbm, hid_out, grad_out,
    tok, codes, scales, cots, tb, tail, wb, w_other, ct, cot_send, hb, hid_keep, hid_recv, both, dbt, rs_send, rs_recv,
    fin_send, fin_recv, in_sem, out_sem, sent_sem, a_r, b_r, sib_r, y_r, one_r, g_r,
):
    loads = [
        pltpu.make_async_copy(tok_hbm, tok, in_sem.at[0]),
        pltpu.make_async_copy(codes_hbm, codes.at[pl.ds(0, HID)], in_sem.at[1]),
        pltpu.make_async_copy(scales_hbm, scales, in_sem.at[2]),
        pltpu.make_async_copy(cot_hbm, cots, in_sem.at[3]),
    ]
    for c in loads:
        c.start()

    node, local = lax.axis_index("node"), lax.axis_index("local")
    core = lax.rem(node, 2)
    x = lax.rem(lax.div(node, 2), 8)
    z_lo = lax.rem(local, 2)
    z = lax.div(node, 16) * 2 + z_lo
    y = lax.div(local, 2)

    def wrap(v):
        return lax.rem(v + RING, RING)

    def device(cx, cy, cz, cc):
        return (lax.div(cz, 2) * 16 + cx * 2 + cc, cy * 2 + lax.rem(cz, 2))

    first, second = jnp.where(core == 0, x, z), jnp.where(core == 0, z, x)

    def at(a, b):
        return jnp.where(core == 0, a, b), jnp.where(core == 0, b, a)

    def on_first(step):
        cx, cz = at(wrap(first + step), second)
        return device(cx, y, cz, core)

    def on_second(step):
        cx, cz = at(first, wrap(second + step))
        return device(cx, y, cz, core)

    def on_y(step):
        return device(x, wrap(y + step), z, core)

    sibling = device(x, y, z, 1 - core)
    partner = device(x, y, lax.div(z, 2) * 2 + (1 - z_lo), core)

    def block_index(cx, cz, cc):
        return (lax.rem(cz, 2) * 2 + cc) * 32 + lax.div(cz, 2) * 8 + cx

    first_at = {a: wrap(first + a) for a in range(-4, 5)}
    second_at = {b: wrap(second + b) for b in range(-4, 5)}

    def index_of(a, b):
        cx, cz = at(first_at[a], second_at[b])
        return block_index(cx, cz, core)

    def sibling_index(a, b):
        cx, cz = at(first_at[b], second_at[a])
        return block_index(cx, cz, 1 - core)

    def block(index, part=None):
        if part is None:
            return tb.at[index]
        return tb.at[index, pl.ds(0, CUT) if part == 0 else pl.ds(CUT, BLOCK - CUT), :]

    pieces = [0, 0]

    def copy(src, dst, kind, recv_sem, target):
        return pltpu.make_async_remote_copy(
            src_ref=src, dst_ref=dst, send_sem=sent_sem.at[kind], recv_sem=recv_sem, device_id=target,
            device_id_type=MESH,
        )

    def start(c, kind, count=1):
        c.start()
        if kind < 2:
            pieces[kind] += count

    def take(recv_sem, count=1):
        ref = tb.at[pl.ds(0, count)]
        copy(ref, ref, 0, recv_sem, sibling).wait_recv()

    def all_left(kind):
        ref = tb.at[pl.ds(0, round(pieces[kind]))]
        copy(ref, ref, kind, a_r.at[0], sibling).wait_send()

    barrier = pltpu.get_barrier_semaphore()
    peers = [sibling, on_y(1), on_y(-1)]
    for step in (1, -1, 2, -2):
        peers += [on_first(step), on_second(step)]
    for peer in peers:
        pl.semaphore_signal(barrier, inc=1, device_id=peer, device_id_type=MESH)

    own = index_of(0, 0)
    loads[0].wait()
    t = tok[...]
    tb[own, 0:64, :] = t[:, 0:128]
    tb[own, 64:128, :] = t[:, 128:256]
    rest = t[:, 256:352]
    tail[own, :, 0:96] = rest
    r = [rest[16 * i : 16 * i + 16, :] for i in range(4)]
    tb[own, 128:144, :] = jnp.concatenate([r[0], r[1][:, 0:32]], axis=1)
    tb[own, 144:160, :] = jnp.concatenate([r[1][:, 32:96], r[2][:, 0:64]], axis=1)
    tb[own, 160:176, :] = jnp.concatenate([r[2][:, 64:96], r[3]], axis=1)

    codes[HID : 2 * HALF] = jnp.zeros((2 * HALF - HID, 2, KB), BF16)
    loads[1].wait()
    loads[2].wait()
    scale = scales[...].astype(F32)[None]

    def weights(half):
        part = codes[pl.ds(half * HALF, HALF)].astype(F32) * scale
        w = part.reshape(ROWS, KB).astype(BF16)
        return (
            jnp.concatenate([w[:, 0:64], w[:, 128:192]], axis=1),
            jnp.concatenate([w[:, 64:128], w[:, 192:256]], axis=1),
        )

    for h, w in enumerate(weights(1 - z_lo)):
        w_other[h] = w
    pl.semaphore_wait(barrier, len(peers))

    def unpack(q):
        p0, p1, p2 = tb[q, 128:144, :], tb[q, 144:160, :], tb[q, 160:176, :]
        tail[q, 0:16, 0:96] = p0[:, 0:96]
        tail[q, 16:32, 0:96] = jnp.concatenate([p0[:, 96:128], p1[:, 0:64]], axis=1)
        tail[q, 32:48, 0:96] = jnp.concatenate([p1[:, 64:128], p2[:, 0:32]], axis=1)
        tail[q, 48:64, 0:96] = p2[:, 32:128]

    def a_send(way, dist):
        sign = 1 - 2 * way
        if dist <= 2:
            at_a, hops, part = 0, dist, None
        elif dist == 3:
            at_a, hops, part = -2 * sign, 1, None
        else:
            at_a, hops, part = -2 * sign, 2, way
        ref = block(index_of(at_a, 0), part)
        start(copy(ref, ref, 0, a_r.at[dist - 1], on_first(sign * hops)), 0, share_of(dist, way))

    def share_of(step, way):
        return 1 if step < 4 else (CUT if way == 0 else BLOCK - CUT) / BLOCK

    def a_arrives(dist):
        take(a_r.at[dist - 1], 2 if dist < 4 else 1)

    def b_sem(item, step):
        return b_r.at[(item + 3) * 4 + step - 1]

    def b_send(way, item, step):
        sign = 1 - 2 * way
        hops = 2 if (item, step) == (4, 4) else 1
        ref = block(index_of(item, -sign * (step - hops)), way if step == 4 else None)
        start(copy(ref, ref, 0, b_sem(item, step), on_second(sign * hops)), 0, share_of(step, way))

    def b_arrives(item, step):
        take(b_sem(item, step), 2 if step < 4 else 1)

    shared = [[]]
    taken = [0]

    def share(blocks):
        if len(shared[-1]) == 4 or len(shared) == 1 and shared[0] == [(0, 0)]:
            shared.append([])
        for a, b in blocks:
            q = index_of(a, b)
            start(copy(block(q), block(q), 0, sib_r.at[len(shared) - 1], sibling), 0)
            shared[-1].append((a, b))
            if (a, b) != (0, 0):
                unpack(q)

    def take_shared(all_of_them):
        while taken[0] < len(shared) - (0 if all_of_them else 2):
            group = shared[taken[0]]
            take(sib_r.at[taken[0]], len(group))
            for a, b in group:
                unpack(sibling_index(a, b))
            taken[0] += 1

    def y_sem(kind, step, h):
        return y_r.at[(kind * 4 + step - 1) * 2 + h]

    def row_block(kind, offset):
        return 2 * wrap(y + offset) + (z_lo if kind == 0 else 1 - z_lo)

    def y_steps(way, kind):
        return 4 if way == kind else 3

    def y_send(way, kind, step, h):
        sign = 1 - 2 * way
        ref = wb.at[h, row_block(kind, -sign * (step - 1))]
        start(copy(ref, ref, 1, y_sem(kind, step, h), on_y(sign)), 1)

    mine = row_block(0, 0)
    theirs = row_block(1, 0)

    def w_copy(h, dst):
        return copy(w_other.at[h], wb.at[h, dst], 1, one_r.at[h], partner)

    def token_send(what):
        for way in range(2):
            if what[1] == "a":
                a_send(way, what[2])
            else:
                b_send(way, what[2], what[3])

    for what in FIRST:
        token_send(what)
    share([(0, 0)])

    for h in range(2):
        start(w_copy(h, mine), 1)
    for h, w in enumerate(weights(z_lo)):
        wb[h, mine] = w
        for way in range(2):
            y_send(way, 0, 1, h)

    loads[3].wait()
    cot = cots[...].astype(F32)
    low, high = cot[0:HALF], jnp.concatenate([cot[HALF:HID], jnp.zeros((2 * HALF - HID, TOK), F32)], axis=0)
    pad = jnp.zeros((8, TOK), F32)
    ct[z_lo] = jnp.concatenate([jnp.where(z_lo == 0, low, high), pad], axis=0).astype(BF16)
    cot_send[...] = jnp.concatenate([jnp.where(z_lo == 0, high, low), pad], axis=0).astype(BF16)

    for what in STEPS:
        if what[0] == "+":
            token_send(what)
            if what == ("+", "b", 4, 3):
                start(copy(cot_send, ct.at[z_lo], 2, one_r.at[2], partner), 2)
            continue
        if what[1] == "a":
            dist = what[2]
            a_arrives(dist)
            share([(dist, 0), (-dist, 0)] if dist < 4 else [(4, 0)])
        elif what[1] == "b":
            _, _, item, step = what
            b_arrives(item, step)
            share([(item, -step), (item, step)] if step < 4 else [(item, 4)])
        elif what[1] == "w":
            h = what[2]
            take(one_r.at[h])
            for way in range(2):
                y_send(way, 1, 1, h)
        else:
            kind, step, h = (0 if what[1] == "o" else 1), what[2], what[3]
            ways = [way for way in range(2) if step <= y_steps(way, kind)]
            take(y_sem(kind, step, h), len(ways))
            for way in ways:
                if step < y_steps(way, kind):
                    y_send(way, kind, step + 1, h)
        take_shared(False)

    def tokens_of(q, count):
        def stack(parts):
            return jnp.concatenate(parts, axis=0)

        return jnp.concatenate(
            [
                stack([tb[q + i, 0:64, :] for i in range(count)]),
                stack([tb[q + i, 64:128, :] for i in range(count)]),
                stack([tail[q + i, :, 0:96] for i in range(count)]),
            ],
            axis=1,
        )

    def forward(m, cc, acc):
        for j in range(4):
            w = jnp.concatenate([wb[cc, 4 * j + i] for i in range(4)], axis=1)
            acc += jnp.dot(w, tokens_of((m * 2 + cc) * 32 + 8 * j, 8), preferred_element_type=F32)
        return acc

    accs = [forward(m, core, jnp.zeros((ROWS, TOK), F32)) for m in range(2)]
    take_shared(True)
    accs = [forward(m, 1 - core, accs[m]) for m in range(2)]
    copy(cot_send, ct.at[1 - z_lo], 2, one_r.at[2], partner).wait_recv()
    for m in range(2):
        acc = accs[m]
        for t in range(3):
            wide = min(128, TOK - 128 * t)
            both[t, :, 0:wide] = acc[:, 128 * t : 128 * t + wide]
        for t in range(3):
            wide = min(128, TOK - 128 * t)
            gate = both[t, pl.ds(0, HALF, stride=2), :][:, 0:wide]
            up = both[t, pl.ds(1, HALF, stride=2), :][:, 0:wide]
            cot = ct[m, :, 128 * t : 128 * t + wide].astype(F32)[0:HALF]
            sig = jax.nn.sigmoid(gate)
            silu = gate * sig
            hid = jnp.concatenate([silu * up, jnp.zeros((8, wide), F32)], axis=0)
            hb[m, :, 128 * t : 128 * t + wide] = hid.astype(BF16)
            both[t, pl.ds(0, HALF, stride=2), 0:wide] = cot * up * sig * (1.0 + gate * (1.0 - sig))
            both[t, pl.ds(1, HALF, stride=2), 0:wide] = cot * silu
            dbt[m, :, 128 * t : 128 * t + wide] = both[t, :, 0:wide].astype(BF16)

    def partial(offset, kind, h):
        rows = row_block(kind, offset)
        total = jnp.zeros((ROWS, 128), F32)
        for m in range(2):
            total += lax.dot_general(
                dbt[m], tokens_of((m * 2 + h) * 32 + 2 * rows, 2), (((1,), (1,)), ((), ())), preferred_element_type=F32
            )
        return total

    order = {}
    for way in range(2):
        for kind in range(2):
            for step in range(1, y_steps(way, kind) + 1):
                for h in range(2):
                    order[way, kind, step, h] = len(order)

    def g_copy(way, kind, step, h):
        k = order[way, kind, step, h]
        return copy(rs_send.at[k], rs_recv.at[k], 1, g_r.at[k], on_y(1 - 2 * way))

    def arrived(way, kind, step, h):
        g_copy(way, kind, step, h).wait_recv()
        return rs_recv[order[way, kind, step, h]].astype(F32)

    def hop(way, kind, step, h):
        steps = y_steps(way, kind)
        total = partial((1 - 2 * way) * (steps + 1 - step), kind, h)
        if step > 1:
            total += arrived(way, kind, step - 1, h)
        rs_send[order[way, kind, step, h]] = total.astype(BF16)
        start(g_copy(way, kind, step, h), 1)

    up_order = [(kind, step, h) for step in range(1, 5) for kind in (0, 1) for h in (0, 1) if step <= y_steps(0, kind)]
    down_order = [(kind, step, h) for step in range(1, 3) for kind in (1, 0) for h in (0, 1)]
    down_order += [(1, 3, 0), (1, 3, 1), (0, 3, 0), (1, 4, 0), (1, 4, 1), (0, 3, 1)]
    for slot in range(14):
        hop(1, *down_order[slot])
        hop(0, *up_order[slot])
        if slot == 1:
            start(copy(hb.at[1 - z_lo], hid_recv, 3, one_r.at[3], partner), 3)
        if slot == 7:
            copy(hb.at[1 - z_lo], hid_recv, 3, one_r.at[3], partner).wait_recv()
            here = hb[z_lo].astype(F32)
            there = hid_recv[...].astype(F32)
            h_low = jnp.where(z_lo == 0, here, there)[0:HALF]
            h_high = jnp.where(z_lo == 0, there, here)[0 : HID - HALF]
            hid_keep[...] = jnp.concatenate([h_low, h_high], axis=0).astype(BF16)
            hid_copy = pltpu.make_async_copy(hid_keep, hid_out, out_sem.at[0])
            hid_copy.start()

    def fin_copy(h):
        return copy(fin_send.at[h], fin_recv.at[h], 1, one_r.at[4 + h], partner)

    for h in range(2):
        total = partial(0, 1, h)
        total += arrived(0, 1, 3, h)
        total += arrived(1, 1, 4, h)
        fin_send[h] = total.astype(BF16)
        start(fin_copy(h), 1)

    def put(parts, is_low):
        rows = jnp.concatenate(
            [parts[0][:, 0:64], parts[1][:, 0:64], parts[0][:, 64:128], parts[1][:, 64:128]], axis=1
        )

        rows = rows.reshape(HALF, 2, KB)

        @pl.when(is_low)
        def _():
            grad_out[0:HALF] = rows

        @pl.when(jnp.logical_not(is_low))
        def _():
            grad_out[HALF:HID] = rows[0 : HID - HALF]

    finals = []
    for h in range(2):
        total = partial(0, 0, h)
        total += arrived(1, 0, 3, h)
        total += arrived(0, 0, 4, h)
        finals.append(total)
    put(finals, z_lo == 0)
    for h in range(2):
        fin_copy(h).wait_recv()
    put([fin_recv[h].astype(F32) for h in range(2)], z_lo == 1)
    hid_copy.wait()
    for kind in range(2):
        all_left(kind)
    copy(cot_send, ct.at[z_lo], 2, one_r.at[2], partner).wait_send()
    copy(hb.at[1 - z_lo], hid_recv, 3, one_r.at[3], partner).wait_send()


def move(hid_in, grad_in, hid_out, grad_out, hid, grad, sem):
    arrive = [
        pltpu.make_async_copy(grad_in, grad, sem.at[0]),
        pltpu.make_async_copy(hid_in, hid, sem.at[1]),
    ]
    leave = [
        pltpu.make_async_copy(grad, grad_out, sem.at[2]),
        pltpu.make_async_copy(hid, hid_out, sem.at[3]),
    ]
    for c in arrive:
        c.start()
    for k in range(2):
        arrive[k].wait()
        leave[k].start()
    for c in leave:
        c.wait()


def body(tokens, codes, scales, cotangent):
    dma = pltpu.SemaphoreType.DMA
    vmem = pl.BlockSpec(memory_space=pltpu.VMEM)
    hbm = pl.BlockSpec(memory_space=pltpu.HBM)
    out_shape = (jax.ShapeDtypeStruct((HID, TOK), BF16), jax.ShapeDtypeStruct((HID, 2, KB), F32))
    results = pl.pallas_call(
        kernel,
        name="glu",
        out_shape=out_shape,
        in_specs=[hbm] * 4,
        out_specs=(hbm, vmem),
        scratch_shapes=[
            pltpu.VMEM((FEAT, TOK), BF16),
            pltpu.VMEM((2 * HALF, 2, KB), BF16),
            pltpu.VMEM((2, KB), BF16),
            pltpu.VMEM((HID, TOK), BF16),
            pltpu.VMEM((128, BLOCK, 128), BF16),
            pltpu.VMEM((128, FEAT, 128), BF16),
            pltpu.VMEM((2, 16, ROWS, 128), BF16),
            pltpu.VMEM((2, ROWS, 128), BF16),
            pltpu.VMEM((2, 96, TOK), BF16),
            pltpu.VMEM((96, TOK), BF16),
            pltpu.VMEM((2, 96, TOK), BF16),
            pltpu.VMEM((HID, TOK), BF16),
            pltpu.VMEM((96, TOK), BF16),
            pltpu.VMEM((3, ROWS, 128), F32),
            pltpu.VMEM((2, ROWS, TOK), BF16),
            pltpu.VMEM((28, ROWS, 128), BF16),
            pltpu.VMEM((28, ROWS, 128), BF16),
            pltpu.VMEM((2, ROWS, 128), BF16),
            pltpu.VMEM((2, ROWS, 128), BF16),
            dma((4,)), dma((1,)), dma((4,)), dma((4,)), dma((32,)), dma((19,)), dma((16,)), dma((6,)), dma((28,)),
        ],
        compiler_params=pltpu.CompilerParams(
            collective_id=0, has_side_effects=True, vmem_limit_bytes=56 * 2**20
        ),
    )(jnp.transpose(tokens), jnp.transpose(codes, (2, 1, 0)), jnp.transpose(scales), jnp.transpose(cotangent))
    hidden, grads = pl.pallas_call(
        move,
        name="move",
        out_shape=out_shape,
        in_specs=[hbm] * 2,
        out_specs=(hbm, hbm),
        scratch_shapes=[pltpu.VMEM((HID, TOK), BF16), pltpu.VMEM((HID, 2, KB), F32), dma((4,))],
        compiler_params=pltpu.CompilerParams(vmem_limit_bytes=56 * 2**20),
    )(*results)
    return jnp.transpose(hidden), jnp.transpose(grads, (2, 1, 0))


def solution(mesh):
    in_specs = (P("local", "node"), P("local", None, "node"), P("local", None), P("local", "node"))
    out_specs = (P("local", "node"), P("local", None, "node"))
    return jax.shard_map(body, mesh=mesh, in_specs=in_specs, out_specs=out_specs, check_vma=False)
```

time: 323 us -> 71.2 us (0.22)
  the two profiles are of different devices: /device:TPU:4 before, /device:TPU:32 now
where the time goes in v2:
time: 71.2 us; the launch traced here: 71.1 us
  Pallas kernels  70.4 us (99%)
    pallas_call x1, Pallas kernels, body(): pl.pallas_call(kernel, name='glu', out_shape=out_shape, in_specs=[hbm] *...  68.6 us
    pallas_call x1, Pallas kernels, body(): pl.pallas_call(move, name='move', out_shape=out_shape, in_specs=[hbm] * 2...  1.79 us

profile of v2, /device:TPU:32, one launch (start us, length us, event | category | flops | bytes accessed | tf_op | source)
XLA Modules:
  0.0 71.1 jit_solution(123954981170996945)
XLA Ops:
  0.6 68.6 %glu.1 = (bf16[172,352]{1,0:T(8,128)(2,1)}, f32[172,2,256]{2,1,0:T(2,128)}) custom-call(bf16[64,352]{1,0:T(8,128)(2,1)} %bitcast.8, bf16[172,2,256]{2,1,0:T(2,128)(2,1)} %bitcast.6, bf16[2,256]{1,0:T(2,128)(2,1)} %bitcast.9, bf16[172,352]{1,0:T(8,128)(2,1)} %bitcast.7), custom_call_target="tpu_custom_call" | custom-call | tf_op jit(solution)/shard_map/glu/pallas_call | solution.py:451
  69.3 1.8 %move.1 = (bf16[172,352]{1,0:T(8,128)(2,1)}, f32[172,2,256]{2,1,0:T(2,128)}) custom-call(bf16[172,352]{1,0:T(8,128)(2,1)} %get-tuple-element.6.hid_in, f32[172,2,256]{2,1,0:T(2,128)} %get-tuple-element.7.grad_in), custom_call_target="tpu_custom_call" | custom-call | tf_op jit(solution)/shard_map/move/pallas_call | solution.py:483

commit v3 on v2

--- a/solution.py
+++ b/solution.py
@@ -22,27 +22,27 @@
     ("+", "a", 2), ("+", "a", 1), ("+", "b", 0, 1),
 ]
 STEPS = [
-    ("-", "a", 2), ("+", "a", 3), ("+", "a", 4), ("+", "b", 2, 1), ("-", "a", 1), ("-", "w", 0), ("+", "b", -2, 1),
-    ("-", "w", 1), ("+", "b", 1, 1), ("-", "o", 1, 0), ("+", "b", -1, 1), ("-", "b", 0, 1), ("+", "b", 0, 2),
-    ("-", "o", 1, 1), ("-", "a", 3), ("+", "b", 3, 1), ("+", "b", -3, 1), ("-", "a", 4), ("+", "b", 4, 1),
-    ("-", "p", 1, 0), ("-", "b", 2, 1), ("+", "b", 2, 2), ("-", "b", -2, 1), ("+", "b", -2, 2), ("-", "p", 1, 1),
-    ("-", "b", 1, 1), ("+", "b", 1, 2), ("-", "b", -1, 1), ("+", "b", -1, 2), ("-", "o", 2, 0), ("-", "b", 0, 2),
-    ("+", "b", 0, 3), ("-", "b", 3, 1), ("+", "b", 3, 2), ("-", "o", 2, 1), ("-", "b", -3, 1), ("+", "b", -3, 2),
-    ("-", "b", 4, 1), ("+", "b", 4, 2), ("-", "p", 2, 0), ("-", "b", 2, 2), ("+", "b", 2, 3), ("-", "b", -2, 2),
-    ("+", "b", -2, 3), ("-", "p", 2, 1), ("-", "b", 1, 2), ("+", "b", 1, 3), ("-", "b", -1, 2), ("+", "b", -1, 3),
-    ("-", "o", 3, 0), ("-", "b", 0, 3), ("+", "b", 0, 4), ("-", "b", 3, 2), ("+", "b", 3, 3), ("-", "o", 3, 1),
-    ("-", "b", -3, 2), ("+", "b", -3, 3), ("-", "b", 4, 2), ("+", "b", 4, 4), ("+", "b", 4, 3), ("-", "p", 3, 0),
-    ("-", "b", 2, 3), ("+", "b", 2, 4), ("-", "b", -2, 3), ("+", "b", -2, 4), ("-", "p", 3, 1), ("-", "b", 1, 3),
-    ("+", "b", 1, 4), ("-", "b", -1, 3), ("+", "b", -1, 4), ("-", "b", 0, 4), ("-", "o", 4, 0), ("-", "b", 3, 3),
-    ("+", "b", 3, 4), ("-", "b", -3, 3), ("+", "b", -3, 4), ("-", "o", 4, 1), ("-", "p", 4, 0), ("-", "b", 4, 4),
-    ("-", "b", 4, 3), ("-", "b", 2, 4), ("-", "p", 4, 1), ("-", "b", -2, 4), ("-", "b", 1, 4), ("-", "b", -1, 4),
-    ("-", "b", 3, 4), ("-", "b", -3, 4),
+    ("-", "a", 2), ("+", "a", 3), ("+", "a", 4), ("+", "b", 2, 1), ("-", "a", 1), ("+", "b", -2, 1), ("+", "b", 1, 1),
+    ("+", "b", -1, 1), ("-", "b", 0, 1), ("-", "w", 0), ("+", "b", 0, 2), ("-", "w", 1), ("-", "o", 1, 0),
+    ("-", "a", 3), ("+", "b", 3, 1), ("+", "b", -3, 1), ("-", "o", 1, 1), ("-", "a", 4), ("+", "b", 4, 1),
+    ("-", "b", 2, 1), ("+", "b", 2, 2), ("-", "b", -2, 1), ("+", "b", -2, 2), ("-", "b", 1, 1), ("+", "b", 1, 2),
+    ("-", "p", 1, 0), ("-", "b", -1, 1), ("+", "b", -1, 2), ("-", "b", 0, 2), ("+", "b", 0, 3), ("-", "p", 1, 1),
+    ("-", "b", 3, 1), ("+", "b", 3, 2), ("-", "b", -3, 1), ("+", "b", -3, 2), ("-", "o", 2, 0), ("-", "b", 4, 1),
+    ("+", "b", 4, 2), ("-", "b", 2, 2), ("+", "b", 2, 3), ("-", "o", 2, 1), ("-", "b", -2, 2), ("+", "b", -2, 3),
+    ("-", "b", 1, 2), ("+", "b", 1, 3), ("-", "p", 2, 0), ("-", "b", -1, 2), ("+", "b", -1, 3), ("-", "b", 0, 3),
+    ("+", "b", 0, 4), ("-", "p", 2, 1), ("-", "b", 3, 2), ("+", "b", 3, 3), ("-", "b", -3, 2), ("+", "b", -3, 3),
+    ("-", "o", 3, 0), ("-", "b", 4, 2), ("+", "b", 4, 4), ("+", "b", 4, 3), ("-", "b", 2, 3), ("-", "o", 3, 1),
+    ("+", "b", 2, 4), ("-", "b", -2, 3), ("+", "b", -2, 4), ("-", "b", 1, 3), ("+", "b", 1, 4), ("-", "p", 3, 0),
+    ("-", "b", -1, 3), ("+", "b", -1, 4), ("-", "b", 0, 4), ("-", "b", 3, 3), ("+", "b", 3, 4), ("-", "p", 3, 1),
+    ("-", "b", -3, 3), ("+", "b", -3, 4), ("-", "o", 4, 0), ("-", "b", 4, 4), ("-", "b", 4, 3), ("-", "b", 2, 4),
+    ("-", "b", -2, 4), ("-", "o", 4, 1), ("-", "b", 1, 4), ("-", "p", 4, 0), ("-", "b", -1, 4), ("-", "b", 3, 4),
+    ("-", "b", -3, 4), ("-", "p", 4, 1),
 ]
 
 
 def kernel(
     tok_hbm, codes_hbm, scales_hbm, cot_hbm, hid_out, grad_out,
-    tok, codes, scales, cots, tb, tail, wb, w_other, ct, cot_send, hb, hid_keep, hid_recv, both, dbt, rs_send, rs_recv,
+    tok, codes, scales, cots, tb, tail, wb, w_other, ct, cot_send, hb, hid_keep, hid_recv, both, dbt, grad, rs_send, rs_recv,
     fin_send, fin_recv, in_sem, out_sem, sent_sem, a_r, b_r, sib_r, y_r, one_r, g_r,
 ):
     loads = [
@@ -84,7 +84,11 @@
         return device(x, wrap(y + step), z, core)
 
     sibling = device(x, y, z, 1 - core)
-    partner = device(x, y, lax.div(z, 2) * 2 + (1 - z_lo), core)
+    other_z = lax.div(z, 2) * 2 + (1 - z_lo)
+    partner = device(x, y, other_z, core)
+
+    def on_y_partner(step):
+        return device(x, wrap(y + step), other_z, core)
 
     def block_index(cx, cz, cc):
         return (lax.rem(cz, 2) * 2 + cc) * 32 + lax.div(cz, 2) * 8 + cx
@@ -127,7 +131,7 @@
         copy(ref, ref, kind, a_r.at[0], sibling).wait_send()
 
     barrier = pltpu.get_barrier_semaphore()
-    peers = [sibling, on_y(1), on_y(-1)]
+    peers = [sibling, on_y(1), on_y(-1), on_y_partner(1), on_y_partner(-1)]
     for step in (1, -1, 2, -2):
         peers += [on_first(step), on_second(step)]
     for peer in peers:
@@ -351,7 +355,8 @@
 
     def g_copy(way, kind, step, h):
         k = order[way, kind, step, h]
-        return copy(rs_send.at[k], rs_recv.at[k], 1, g_r.at[k], on_y(1 - 2 * way))
+        to = on_y_partner if kind == 1 and step == y_steps(way, kind) else on_y
+        return copy(rs_send.at[k], rs_recv.at[k], 1, g_r.at[k], to(1 - 2 * way))
 
     def arrived(way, kind, step, h):
         g_copy(way, kind, step, h).wait_recv()
@@ -364,6 +369,9 @@
             total += arrived(way, kind, step - 1, h)
         rs_send[order[way, kind, step, h]] = total.astype(BF16)
         start(g_copy(way, kind, step, h), 1)
+
+    def fin_copy(h):
+        return copy(fin_send.at[h], fin_recv.at[h], 1, one_r.at[4 + h], partner)
 
     up_order = [(kind, step, h) for step in range(1, 5) for kind in (0, 1) for h in (0, 1) if step <= y_steps(0, kind)]
     down_order = [(kind, step, h) for step in range(1, 3) for kind in (1, 0) for h in (0, 1)]
@@ -373,6 +381,9 @@
         hop(0, *up_order[slot])
         if slot == 1:
             start(copy(hb.at[1 - z_lo], hid_recv, 3, one_r.at[3], partner), 3)
+        if slot in (4, 5):
+            fin_send[slot - 4] = partial(0, 1, slot - 4).astype(BF16)
+            start(fin_copy(slot - 4), 1)
         if slot == 7:
             copy(hb.at[1 - z_lo], hid_recv, 3, one_r.at[3], partner).wait_recv()
             here = hb[z_lo].astype(F32)
@@ -383,16 +394,6 @@
             hid_copy = pltpu.make_async_copy(hid_keep, hid_out, out_sem.at[0])
             hid_copy.start()
 
-    def fin_copy(h):
-        return copy(fin_send.at[h], fin_recv.at[h], 1, one_r.at[4 + h], partner)
-
-    for h in range(2):
-        total = partial(0, 1, h)
-        total += arrived(0, 1, 3, h)
-        total += arrived(1, 1, 4, h)
-        fin_send[h] = total.astype(BF16)
-        start(fin_copy(h), 1)
-
     def put(parts, is_low):
         rows = jnp.concatenate(
             [parts[0][:, 0:64], parts[1][:, 0:64], parts[0][:, 64:128], parts[1][:, 64:128]], axis=1
@@ -402,22 +403,27 @@
 
         @pl.when(is_low)
         def _():
-            grad_out[0:HALF] = rows
+            grad[0:HALF] = rows
+            grad_copies[0].start()
 
         @pl.when(jnp.logical_not(is_low))
         def _():
-            grad_out[HALF:HID] = rows[0 : HID - HALF]
-
-    finals = []
-    for h in range(2):
-        total = partial(0, 0, h)
-        total += arrived(1, 0, 3, h)
-        total += arrived(0, 0, 4, h)
-        finals.append(total)
-    put(finals, z_lo == 0)
+            grad[HALF:HID] = rows[0 : HID - HALF]
+            grad_copies[1].start()
+
+    grad_copies = [
+        pltpu.make_async_copy(grad.at[pl.ds(lo, n)], grad_out.at[pl.ds(lo, n)], out_sem.at[k])
+        for k, lo, n in ((1, 0, HALF), (2, HALF, HID - HALF))
+    ]
+    own_terms = [partial(0, 0, h) for h in range(2)]
+    others = []
     for h in range(2):
         fin_copy(h).wait_recv()
-    put([fin_recv[h].astype(F32) for h in range(2)], z_lo == 1)
+        others.append(fin_recv[h].astype(F32) + arrived(0, 1, 3, h) + arrived(1, 1, 4, h))
+    put(others, z_lo == 1)
+    put([own_terms[h] + arrived(1, 0, 3, h) + arrived(0, 0, 4, h) for h in range(2)], z_lo == 0)
+    for c in grad_copies:
+        c.wait()
     hid_copy.wait()
     for kind in range(2):
         all_left(kind)
@@ -445,7 +451,6 @@
 
 def body(tokens, codes, scales, cotangent):
     dma = pltpu.SemaphoreType.DMA
-    vmem = pl.BlockSpec(memory_space=pltpu.VMEM)
     hbm = pl.BlockSpec(memory_space=pltpu.HBM)
     out_shape = (jax.ShapeDtypeStruct((HID, TOK), BF16), jax.ShapeDtypeStruct((HID, 2, KB), F32))
     results = pl.pallas_call(
@@ -453,7 +458,7 @@
         name="glu",
         out_shape=out_shape,
         in_specs=[hbm] * 4,
-        out_specs=(hbm, vmem),
+        out_specs=(hbm, hbm),
         scratch_shapes=[
             pltpu.VMEM((FEAT, TOK), BF16),
             pltpu.VMEM((2 * HALF, 2, KB), BF16),
@@ -470,11 +475,12 @@
             pltpu.VMEM((96, TOK), BF16),
             pltpu.VMEM((3, ROWS, 128), F32),
             pltpu.VMEM((2, ROWS, TOK), BF16),
+            pltpu.VMEM((HID, 2, KB), F32),
             pltpu.VMEM((28, ROWS, 128), BF16),
             pltpu.VMEM((28, ROWS, 128), BF16),
             pltpu.VMEM((2, ROWS, 128), BF16),
             pltpu.VMEM((2, ROWS, 128), BF16),
-            dma((4,)), dma((1,)), dma((4,)), dma((4,)), dma((32,)), dma((19,)), dma((16,)), dma((6,)), dma((28,)),
+            dma((4,)), dma((3,)), dma((4,)), dma((4,)), dma((32,)), dma((19,)), dma((16,)), dma((6,)), dma((28,)),
         ],
         compiler_params=pltpu.CompilerParams(
             collective_id=0, has_side_effects=True, vmem_limit_bytes=56 * 2**20

time: 71.2 us -> 70 us (0.983)
  the two profiles are of different devices: /device:TPU:32 before, /device:TPU:2 now
where the time goes in v3:
time: 70 us; the launch traced here: 69.8 us
  Pallas kernels  69.1 us (99%)
    pallas_call x1, Pallas kernels, body(): pl.pallas_call(kernel, name='glu', out_shape=out_shape, in_specs=[hbm] *...  67.3 us
    pallas_call x1, Pallas kernels, body(): pl.pallas_call(move, name='move', out_shape=out_shape, in_specs=[hbm] * 2...  1.79 us

profile of v3, /device:TPU:2, one launch (start us, length us, event | category | flops | bytes accessed | tf_op | source)
XLA Modules:
  0.0 69.8 jit_solution(14460302341562386675)
XLA Ops:
  0.6 67.3 %glu.1 = (bf16[172,352]{1,0:T(8,128)(2,1)}, f32[172,2,256]{2,1,0:T(2,128)}) custom-call(bf16[64,352]{1,0:T(8,128)(2,1)} %bitcast.8, bf16[172,2,256]{2,1,0:T(2,128)(2,1)} %bitcast.6, bf16[2,256]{1,0:T(2,128)(2,1)} %bitcast.9, bf16[172,352]{1,0:T(8,128)(2,1)} %bitcast.7), custom_call_target="tpu_custom_call" | custom-call | tf_op jit(solution)/shard_map/glu/pallas_call | solution.py:456
  68.0 1.8 %move.1 = (bf16[172,352]{1,0:T(8,128)(2,1)}, f32[172,2,256]{2,1,0:T(2,128)}) custom-call(bf16[172,352]{1,0:T(8,128)(2,1)} %get-tuple-element.6.hid_in, f32[172,2,256]{2,1,0:T(2,128)} %get-tuple-element.7.grad_in), custom_call_target="tpu_custom_call" | custom-call | tf_op jit(solution)/shard_map/move/pallas_call | solution.py:489

commit v4 on v3

--- a/solution.py
+++ b/solution.py
@@ -268,10 +268,11 @@
     ct[z_lo] = jnp.concatenate([jnp.where(z_lo == 0, low, high), pad], axis=0).astype(BF16)
     cot_send[...] = jnp.concatenate([jnp.where(z_lo == 0, high, low), pad], axis=0).astype(BF16)
 
+    last_send = [what for what in STEPS if what[0] == "+"][-1]
     for what in STEPS:
         if what[0] == "+":
             token_send(what)
-            if what == ("+", "b", 4, 3):
+            if what == last_send:
                 start(copy(cot_send, ct.at[z_lo], 2, one_r.at[2], partner), 2)
             continue
         if what[1] == "a":

time: 70 us -> 69.9 us (level)
  no operation moved by 1% of the time
where the time goes in v4:
time: 69.9 us; the launch traced here: 69.6 us
  Pallas kernels  69 us (99%)
    pallas_call x1, Pallas kernels, body(): pl.pallas_call(kernel, name='glu', out_shape=out_shape, in_specs=[hbm] *...  67.2 us
    pallas_call x1, Pallas kernels, body(): pl.pallas_call(move, name='move', out_shape=out_shape, in_specs=[hbm] * 2...  1.79 us

profile of v4, /device:TPU:2, one launch (start us, length us, event | category | flops | bytes accessed | tf_op | source)
XLA Modules:
  0.0 69.6 jit_solution(2353696610187618970)
XLA Ops:
  0.6 67.2 %glu.1 = (bf16[172,352]{1,0:T(8,128)(2,1)}, f32[172,2,256]{2,1,0:T(2,128)}) custom-call(bf16[64,352]{1,0:T(8,128)(2,1)} %bitcast.8, bf16[172,2,256]{2,1,0:T(2,128)(2,1)} %bitcast.6, bf16[2,256]{1,0:T(2,128)(2,1)} %bitcast.9, bf16[172,352]{1,0:T(8,128)(2,1)} %bitcast.7), custom_call_target="tpu_custom_call" | custom-call | tf_op jit(solution)/shard_map/glu/pallas_call | solution.py:457
  67.8 1.8 %move.1 = (bf16[172,352]{1,0:T(8,128)(2,1)}, f32[172,2,256]{2,1,0:T(2,128)}) custom-call(bf16[172,352]{1,0:T(8,128)(2,1)} %get-tuple-element.6.hid_in, f32[172,2,256]{2,1,0:T(2,128)} %get-tuple-element.7.grad_in), custom_call_target="tpu_custom_call" | custom-call | tf_op jit(solution)/shard_map/move/pallas_call | solution.py:490

commit v5 on v4

--- a/solution.py
+++ b/solution.py
@@ -148,22 +148,6 @@
     tb[own, 128:144, :] = jnp.concatenate([r[0], r[1][:, 0:32]], axis=1)
     tb[own, 144:160, :] = jnp.concatenate([r[1][:, 32:96], r[2][:, 0:64]], axis=1)
     tb[own, 160:176, :] = jnp.concatenate([r[2][:, 64:96], r[3]], axis=1)
-
-    codes[HID : 2 * HALF] = jnp.zeros((2 * HALF - HID, 2, KB), BF16)
-    loads[1].wait()
-    loads[2].wait()
-    scale = scales[...].astype(F32)[None]
-
-    def weights(half):
-        part = codes[pl.ds(half * HALF, HALF)].astype(F32) * scale
-        w = part.reshape(ROWS, KB).astype(BF16)
-        return (
-            jnp.concatenate([w[:, 0:64], w[:, 128:192]], axis=1),
-            jnp.concatenate([w[:, 64:128], w[:, 192:256]], axis=1),
-        )
-
-    for h, w in enumerate(weights(1 - z_lo)):
-        w_other[h] = w
     pl.semaphore_wait(barrier, len(peers))
 
     def unpack(q):
@@ -254,7 +238,21 @@
         token_send(what)
     share([(0, 0)])
 
-    for h in range(2):
+    codes[HID : 2 * HALF] = jnp.zeros((2 * HALF - HID, 2, KB), BF16)
+    loads[1].wait()
+    loads[2].wait()
+    scale = scales[...].astype(F32)[None]
+
+    def weights(half):
+        part = codes[pl.ds(half * HALF, HALF)].astype(F32) * scale
+        w = part.reshape(ROWS, KB).astype(BF16)
+        return (
+            jnp.concatenate([w[:, 0:64], w[:, 128:192]], axis=1),
+            jnp.concatenate([w[:, 64:128], w[:, 192:256]], axis=1),
+        )
+
+    for h, w in enumerate(weights(1 - z_lo)):
+        w_other[h] = w
         start(w_copy(h, mine), 1)
     for h, w in enumerate(weights(z_lo)):
         wb[h, mine] = w

time: 69.9 us -> 69.8 us (level)
  no operation moved by 1% of the time
where the time goes in v5:
time: 69.8 us; the launch traced here: 69.6 us
  Pallas kernels  69 us (99%)
    pallas_call x1, Pallas kernels, body(): pl.pallas_call(kernel, name='glu', out_shape=out_shape, in_specs=[hbm] *...  67.2 us
    pallas_call x1, Pallas kernels, body(): pl.pallas_call(move, name='move', out_shape=out_shape, in_specs=[hbm] * 2...  1.79 us

profile of v5, /device:TPU:2, one launch (start us, length us, event | category | flops | bytes accessed | tf_op | source)
XLA Modules:
  0.0 69.6 jit_solution(17020978708372587891)
XLA Ops:
  0.6 67.2 %glu.1 = (bf16[172,352]{1,0:T(8,128)(2,1)}, f32[172,2,256]{2,1,0:T(2,128)}) custom-call(bf16[64,352]{1,0:T(8,128)(2,1)} %bitcast.8, bf16[172,2,256]{2,1,0:T(2,128)(2,1)} %bitcast.6, bf16[2,256]{1,0:T(2,128)(2,1)} %bitcast.9, bf16[172,352]{1,0:T(8,128)(2,1)} %bitcast.7), custom_call_target="tpu_custom_call" | custom-call | tf_op jit(solution)/shard_map/glu/pallas_call | solution.py:455
  67.8 1.8 %move.1 = (bf16[172,352]{1,0:T(8,128)(2,1)}, f32[172,2,256]{2,1,0:T(2,128)}) custom-call(bf16[172,352]{1,0:T(8,128)(2,1)} %get-tuple-element.6.hid_in, f32[172,2,256]{2,1,0:T(2,128)} %get-tuple-element.7.grad_in), custom_call_target="tpu_custom_call" | custom-call | tf_op jit(solution)/shard_map/move/pallas_call | solution.py:488

commit v6 on v5

--- a/solution.py
+++ b/solution.py
@@ -23,20 +23,20 @@
 ]
 STEPS = [
     ("-", "a", 2), ("+", "a", 3), ("+", "a", 4), ("+", "b", 2, 1), ("-", "a", 1), ("+", "b", -2, 1), ("+", "b", 1, 1),
-    ("+", "b", -1, 1), ("-", "b", 0, 1), ("-", "w", 0), ("+", "b", 0, 2), ("-", "w", 1), ("-", "o", 1, 0),
-    ("-", "a", 3), ("+", "b", 3, 1), ("+", "b", -3, 1), ("-", "o", 1, 1), ("-", "a", 4), ("+", "b", 4, 1),
+    ("+", "b", -1, 1), ("-", "b", 0, 1), ("+", "b", 0, 2), ("-", "w"),
+    ("-", "a", 3), ("+", "b", 3, 1), ("+", "b", -3, 1), ("-", "o", 1), ("-", "a", 4), ("+", "b", 4, 1),
     ("-", "b", 2, 1), ("+", "b", 2, 2), ("-", "b", -2, 1), ("+", "b", -2, 2), ("-", "b", 1, 1), ("+", "b", 1, 2),
-    ("-", "p", 1, 0), ("-", "b", -1, 1), ("+", "b", -1, 2), ("-", "b", 0, 2), ("+", "b", 0, 3), ("-", "p", 1, 1),
-    ("-", "b", 3, 1), ("+", "b", 3, 2), ("-", "b", -3, 1), ("+", "b", -3, 2), ("-", "o", 2, 0), ("-", "b", 4, 1),
-    ("+", "b", 4, 2), ("-", "b", 2, 2), ("+", "b", 2, 3), ("-", "o", 2, 1), ("-", "b", -2, 2), ("+", "b", -2, 3),
-    ("-", "b", 1, 2), ("+", "b", 1, 3), ("-", "p", 2, 0), ("-", "b", -1, 2), ("+", "b", -1, 3), ("-", "b", 0, 3),
-    ("+", "b", 0, 4), ("-", "p", 2, 1), ("-", "b", 3, 2), ("+", "b", 3, 3), ("-", "b", -3, 2), ("+", "b", -3, 3),
-    ("-", "o", 3, 0), ("-", "b", 4, 2), ("+", "b", 4, 4), ("+", "b", 4, 3), ("-", "b", 2, 3), ("-", "o", 3, 1),
-    ("+", "b", 2, 4), ("-", "b", -2, 3), ("+", "b", -2, 4), ("-", "b", 1, 3), ("+", "b", 1, 4), ("-", "p", 3, 0),
-    ("-", "b", -1, 3), ("+", "b", -1, 4), ("-", "b", 0, 4), ("-", "b", 3, 3), ("+", "b", 3, 4), ("-", "p", 3, 1),
-    ("-", "b", -3, 3), ("+", "b", -3, 4), ("-", "o", 4, 0), ("-", "b", 4, 4), ("-", "b", 4, 3), ("-", "b", 2, 4),
-    ("-", "b", -2, 4), ("-", "o", 4, 1), ("-", "b", 1, 4), ("-", "p", 4, 0), ("-", "b", -1, 4), ("-", "b", 3, 4),
-    ("-", "b", -3, 4), ("-", "p", 4, 1),
+    ("-", "b", -1, 1), ("+", "b", -1, 2), ("-", "b", 0, 2), ("+", "b", 0, 3), ("-", "p", 1),
+    ("-", "b", 3, 1), ("+", "b", 3, 2), ("-", "b", -3, 1), ("+", "b", -3, 2), ("-", "b", 4, 1),
+    ("+", "b", 4, 2), ("-", "b", 2, 2), ("+", "b", 2, 3), ("-", "o", 2), ("-", "b", -2, 2), ("+", "b", -2, 3),
+    ("-", "b", 1, 2), ("+", "b", 1, 3), ("-", "b", -1, 2), ("+", "b", -1, 3), ("-", "b", 0, 3),
+    ("+", "b", 0, 4), ("-", "p", 2), ("-", "b", 3, 2), ("+", "b", 3, 3), ("-", "b", -3, 2), ("+", "b", -3, 3),
+    ("-", "b", 4, 2), ("+", "b", 4, 4), ("+", "b", 4, 3), ("-", "b", 2, 3), ("-", "o", 3),
+    ("+", "b", 2, 4), ("-", "b", -2, 3), ("+", "b", -2, 4), ("-", "b", 1, 3), ("+", "b", 1, 4),
+    ("-", "b", -1, 3), ("+", "b", -1, 4), ("-", "b", 0, 4), ("-", "b", 3, 3), ("+", "b", 3, 4), ("-", "p", 3),
+    ("-", "b", -3, 3), ("+", "b", -3, 4), ("-", "b", 4, 4), ("-", "b", 4, 3), ("-", "b", 2, 4),
+    ("-", "b", -2, 4), ("-", "o", 4), ("-", "b", 1, 4), ("-", "b", -1, 4), ("-", "b", 3, 4),
+    ("-", "b", -3, 4), ("-", "p", 4),
 ]
 
 
@@ -207,8 +207,8 @@
                 unpack(sibling_index(a, b))
             taken[0] += 1
 
-    def y_sem(kind, step, h):
-        return y_r.at[(kind * 4 + step - 1) * 2 + h]
+    def y_sem(kind, step):
+        return y_r.at[kind * 4 + step - 1]
 
     def row_block(kind, offset):
         return 2 * wrap(y + offset) + (z_lo if kind == 0 else 1 - z_lo)
@@ -216,16 +216,16 @@
     def y_steps(way, kind):
         return 4 if way == kind else 3
 
-    def y_send(way, kind, step, h):
+    def y_send(way, kind, step):
         sign = 1 - 2 * way
-        ref = wb.at[h, row_block(kind, -sign * (step - 1))]
-        start(copy(ref, ref, 1, y_sem(kind, step, h), on_y(sign)), 1)
+        ref = wb.at[row_block(kind, -sign * (step - 1))]
+        start(copy(ref, ref, 1, y_sem(kind, step), on_y(sign)), 1, 2)
 
     mine = row_block(0, 0)
     theirs = row_block(1, 0)
 
-    def w_copy(h, dst):
-        return copy(w_other.at[h], wb.at[h, dst], 1, one_r.at[h], partner)
+    def w_copy(dst):
+        return copy(w_other, wb.at[dst], 1, one_r.at[0], partner)
 
     def token_send(what):
         for way in range(2):
@@ -253,11 +253,11 @@
 
     for h, w in enumerate(weights(1 - z_lo)):
         w_other[h] = w
-        start(w_copy(h, mine), 1)
+    start(w_copy(mine), 1, 2)
     for h, w in enumerate(weights(z_lo)):
-        wb[h, mine] = w
-        for way in range(2):
-            y_send(way, 0, 1, h)
+        wb[mine, h] = w
+    for way in range(2):
+        y_send(way, 0, 1)
 
     loads[3].wait()
     cot = cots[...].astype(F32)
@@ -282,17 +282,16 @@
             b_arrives(item, step)
             share([(item, -step), (item, step)] if step < 4 else [(item, 4)])
         elif what[1] == "w":
-            h = what[2]
-            take(one_r.at[h])
+            take(one_r.at[0], 2)
             for way in range(2):
-                y_send(way, 1, 1, h)
+                y_send(way, 1, 1)
         else:
-            kind, step, h = (0 if what[1] == "o" else 1), what[2], what[3]
+            kind, step = (0 if what[1] == "o" else 1), what[2]
             ways = [way for way in range(2) if step <= y_steps(way, kind)]
-            take(y_sem(kind, step, h), len(ways))
+            take(y_sem(kind, step), 2 * len(ways))
             for way in ways:
                 if step < y_steps(way, kind):
-                    y_send(way, kind, step + 1, h)
+                    y_send(way, kind, step + 1)
         take_shared(False)
 
     def tokens_of(q, count):
@@ -310,7 +309,7 @@
 
     def forward(m, cc, acc):
         for j in range(4):
-            w = jnp.concatenate([wb[cc, 4 * j + i] for i in range(4)], axis=1)
+            w = jnp.concatenate([wb[4 * j + i, cc] for i in range(4)], axis=1)
             acc += jnp.dot(w, tokens_of((m * 2 + cc) * 32 + 8 * j, 8), preferred_element_type=F32)
         return acc
 
@@ -465,7 +464,7 @@
             pltpu.VMEM((HID, TOK), BF16),
             pltpu.VMEM((128, BLOCK, 128), BF16),
             pltpu.VMEM((128, FEAT, 128), BF16),
-            pltpu.VMEM((2, 16, ROWS, 128), BF16),
+            pltpu.VMEM((16, 2, ROWS, 128), BF16),
             pltpu.VMEM((2, ROWS, 128), BF16),
             pltpu.VMEM((2, 96, TOK), BF16),
             pltpu.VMEM((96, TOK), BF16),
@@ -479,7 +478,7 @@
             pltpu.VMEM((28, ROWS, 128), BF16),
             pltpu.VMEM((2, ROWS, 128), BF16),
             pltpu.VMEM((2, ROWS, 128), BF16),
-            dma((4,)), dma((3,)), dma((4,)), dma((4,)), dma((32,)), dma((19,)), dma((16,)), dma((6,)), dma((28,)),
+            dma((4,)), dma((3,)), dma((4,)), dma((4,)), dma((32,)), dma((19,)), dma((8,)), dma((6,)), dma((28,)),
         ],
         compiler_params=pltpu.CompilerParams(
             collective_id=0, has_side_effects=True, vmem_limit_bytes=56 * 2**20

time: 69.8 us -> 70.1 us (level)
  no operation moved by 1% of the time
where the time goes in v6:
time: 70.1 us; the launch traced here: 70 us
  Pallas kernels  69.3 us (99%)
    pallas_call x1, Pallas kernels, body(): pl.pallas_call(kernel, name='glu', out_shape=out_shape, in_specs=[hbm] *...  67.5 us
    pallas_call x1, Pallas kernels, body(): pl.pallas_call(move, name='move', out_shape=out_shape, in_specs=[hbm] * 2...  1.79 us

profile of v6, /device:TPU:2, one launch (start us, length us, event | category | flops | bytes accessed | tf_op | source)
XLA Modules:
  0.0 70.0 jit_solution(5682017686935382321)
XLA Ops:
  0.6 67.5 %glu.1 = (bf16[172,352]{1,0:T(8,128)(2,1)}, f32[172,2,256]{2,1,0:T(2,128)}) custom-call(bf16[64,352]{1,0:T(8,128)(2,1)} %bitcast.8, bf16[172,2,256]{2,1,0:T(2,128)(2,1)} %bitcast.6, bf16[2,256]{1,0:T(2,128)(2,1)} %bitcast.9, bf16[172,352]{1,0:T(8,128)(2,1)} %bitcast.7), custom_call_target="tpu_custom_call" | custom-call | tf_op jit(solution)/shard_map/glu/pallas_call | solution.py:454
  68.2 1.8 %move.1 = (bf16[172,352]{1,0:T(8,128)(2,1)}, f32[172,2,256]{2,1,0:T(2,128)}) custom-call(bf16[172,352]{1,0:T(8,128)(2,1)} %get-tuple-element.6.hid_in, f32[172,2,256]{2,1,0:T(2,128)} %get-tuple-element.7.grad_in), custom_call_target="tpu_custom_call" | custom-call | tf_op jit(solution)/shard_map/move/pallas_call | solution.py:487
